TPU v7x, 32 devices: a whole 2x2x4 slice. The times are simulated.
32 devices in a mesh: job: 2 (over y), seg: 4 (over x, core), blk: 4 (over z).
Axes of the slice: x: 2, y: 2, z: 4, core: 2. Of those that a mesh axis runs over, the one named last changes fastest.
Arguments:
- amplitudes: float32 [8, 16, 128, 128], P(('job', 'seg'), 'blk'), parts along dimension 0, may hold values from -11 to 11, as said below
- left_env: float32 [8, 16, 128, 128], P(('job', 'seg'), 'blk'), parts along dimension 0, may hold values from -2 to 6, as said below
- right_env: float32 [8, 16, 128, 128], P(('job', 'seg'), 'blk'), parts along dimension 0, may hold values from -2 to 6, as said below
- hop_left: bfloat16 [8, 16, 12, 128, 128], P(('job', 'seg'), 'blk'), parts along dimension 0, may hold values from -0.5 to 0.5
- hop_right: bfloat16 [8, 16, 12, 128, 128], P(('job', 'seg'), 'blk'), parts along dimension 0, may hold values from -0.5 to 0.5
- charges: int32 [32, 2], P('job'), parts along dimension 0, may hold values from -6 to 6
- block_dims: int32 [32, 2], P(('job', 'blk')), parts along dimension 0, may hold values from 64 to 128, as said below
- kept_states: int32 [32], P(('job', 'blk')), parts along dimension 0, may hold values from 32 to 64
- fetch_table: int32 [8, 4, 2], P('job'), parts along dimension 0, may hold values from -1 to 3, as said below
- term_slots: int32 [32, 12], P(('job', 'blk')), parts along dimension 0, may hold values from 0 to 7, as said below
Outputs:
- wave: float32 [8, 16, 128, 128], P(('job', 'seg'), 'blk'), parts along dimension 0
- boundary_env: float32 [8, 16, 128, 128], P(('job', 'seg'), 'blk'), parts along dimension 0
- energies: float32 [8, 2], P(('job', 'seg')), parts along dimension 0
There are 2 independent parts, one for each index of `job`. A program takes and returns all parts, laid end to end along the dimension named above; each array names one. Nothing has to cross between parts.
Inputs may be any that keep to these rules, and one draw needn't show every extreme that they name: `amplitudes`: values of either sign, scaled by a factor per block that differs between blocks, and in some draws also by a factor per row. `left_env`: each block is symmetric. `right_env`: each block is symmetric. `block_dims`: some block has 128 live rows and some block 128 live columns. fetch_table[e, d, c] is the index, within device d's 4 blocks, of the block that fills slot d * 2 + c of device e, and -1 exactly where no hopping term of device e names that slot; the slots of one source device name different blocks; on every device both slots of some source device are named. term_slots[b, k] names a slot of the device that holds block b (blocks b with equal b // 4); the slot's source device is the slot // 2.
All inputs are finite; a program needn't handle non-finite values.
Results may differ from a plain program's by a relative error of at most 0.005.
Values may be sent and summed in bfloat16 or wider, within the bound.
A program may use at most 64 MiB of HBM per device.

v0:
```python
import jax
import jax.numpy as jnp
from jax import lax
from jax.sharding import PartitionSpec as P

ITERS = 2


STEP_SIZE = 0.5
ZEEMAN = 0.5
EPSILON = 1e-06
HIGHEST = lax.Precision.HIGHEST


def for_sending(shard):

    def short(part):
        return part.astype(jnp.bfloat16) if part.dtype == jnp.float32 else part

    return jax.tree.map(short, shard)


def shifted(shard, axis, by):
    peers = lax.axis_size(axis)
    pairs = [(i, i + by) for i in range(peers) if 0 <= i + by < peers]
    return lax.ppermute(shard, axis, pairs)


def on_device(
    amplitudes,
    left_env,
    right_env,
    hop_left,
    hop_right,
    charges,
    block_dims,
    kept_states,
    fetch_table,
    term_slots,
):
    my_index = lax.axis_index("blk")
    devices_blk = lax.axis_size("blk")
    blocks_here = amplitudes.shape[1]
    block_dim = amplitudes.shape[2]
    slot_cap = fetch_table.shape[2]
    entries = float(devices_blk * blocks_here * block_dim * block_dim)
    my_fetch = lax.dynamic_index_in_dim(fetch_table, my_index, 0, keepdims=False)
    source = term_slots // slot_cap
    within = term_slots % slot_cap
    partner = source * blocks_here + my_fetch[source, within]
    parity = (1 - 2 * jnp.remainder(charges[partner, 0], 2)).astype(jnp.float32)
    charges_here = lax.dynamic_slice_in_dim(charges, my_index * blocks_here, blocks_here, 0)
    zeeman_term = (ZEEMAN * charges_here[:, 1].astype(jnp.float32))[:, None, None]
    positions = jnp.arange(block_dim, dtype=jnp.int32)
    live_mask = (
        (positions[None, :, None] < block_dims[:, 0, None, None])
        & (positions[None, None, :] < block_dims[:, 1, None, None])
    ).astype(jnp.float32)
    left_own = left_env[0]
    right_own = right_env[0]
    hop_l = hop_left[0]
    hop_r = hop_right[0]

    def partners_of(amp_half):
        every_block = lax.all_gather(amp_half, "blk", axis=0, tiled=True)
        return every_block[partner]

    def apply_ham(current, left_one):
        amp_half = current.astype(jnp.bfloat16)
        gathered = partners_of(amp_half)
        inner = jnp.einsum(
            "bkij,bkjl->bkil", hop_l, gathered, preferred_element_type=jnp.float32
        ).astype(jnp.bfloat16)
        outer = jnp.einsum("bkij,bkjl->bkil", inner, hop_r, preferred_element_type=jnp.float32)
        hopping = jnp.sum(outer * parity[:, :, None, None], axis=1)
        local_part = jnp.einsum("bij,bjl->bil", left_one, current, precision=HIGHEST)
        local_part = local_part + jnp.einsum("bij,bjl->bil", current, right_own, precision=HIGHEST)
        return live_mask * (local_part + zeeman_term * current + hopping)

    def global_squares(values):
        return lax.psum(jnp.sum(values * values), "blk")

    def davidson(start, left_one):
        diag_sum = (
            jnp.diagonal(left_one, axis1=1, axis2=2)[:, :, None]
            + jnp.diagonal(right_own, axis1=1, axis2=2)[:, None, :]
            + zeeman_term
        )
        current = live_mask * start
        current = current * lax.rsqrt(global_squares(current) / entries + EPSILON)
        energy = jnp.float32(0.0)
        for iteration in range(ITERS):
            image = apply_ham(current, left_one)
            energy = lax.psum(jnp.sum(current * image), "blk") / entries
            correction = live_mask * (image - energy * current) / (1.0 + jnp.abs(diag_sum - energy))
            trial = current - STEP_SIZE * correction
            current = trial * lax.rsqrt(global_squares(trial) / entries + EPSILON)
        return (current, energy)

    updated, first_energy = davidson(amplitudes[0], left_own)
    kept_mask = (positions[None, None, :] < kept_states[:, None, None]).astype(jnp.float32)
    truncated = updated * kept_mask
    carried = jnp.einsum("bij,bjl->bil", left_own, truncated, precision=HIGHEST)
    outgoing_env = jnp.einsum("bji,bjl->bil", truncated, carried, precision=HIGHEST) / block_dim
    incoming = shifted(for_sending(outgoing_env), "seg", 1).astype(outgoing_env.dtype)
    final_wave, second_energy = davidson(updated, left_own + incoming)
    energies = jnp.stack([first_energy, second_energy])[None, :]
    return (final_wave[None], outgoing_env[None], energies)


def solution(mesh):
    placed = (
        P(("job", "seg"), "blk", None, None),
        P(("job", "seg"), "blk", None, None),
        P(("job", "seg"), "blk", None, None),
        P(("job", "seg"), "blk", None, None, None),
        P(("job", "seg"), "blk", None, None, None),
        P("job", None),
        P(("job", "blk"), None),
        P(("job", "blk")),
        P("job", None, None),
        P(("job", "blk"), None),
    )
    return jax.shard_map(
        on_device,
        mesh=mesh,
        in_specs=placed,
        out_specs=(
            P(("job", "seg"), "blk", None, None),
            P(("job", "seg"), "blk", None, None),
            P(("job", "seg"), None),
        ),
        check_vma=False,
    )
```

profile of v0, /device:TPU:0, one launch (start us, length us, event | category | flops | bytes accessed | tf_op | source)
XLA Modules:
  0.0 238.8 jit_solution(14142487167393993616)
XLA Ops:
  0.7 0.9 constant_dynamic-slice_fusion
  1.6 5.8 %copy.62 = f32[1,4,128,128]{1,3,2,0:T(8,128)} copy(f32[1,4,128,128]{3,2,1,0:T(8,128)} %param.12) | data formatting | bytes 524288 | tf_op args[2]
  7.4 0.1 copy.61
  7.5 1.8 gather_fusion.4
  9.4 0.7 multiply_reduce_fusion.13
  10.2 14.1 %psum.70 = f32[]{:T(128)} all-reduce(f32[]{:T(128)} %multiply_reduce_fusion.13), channel_id=1, replica_groups=mesh['job'=2,'seg'=4,'blk'=4] {'blk'}, use_global_device_ids=true, to_apply=%region_1.2 | all-reduce | flops 1 | bytes 8 | tf_op jit(solution)/shard_map/psum | solution.py:81
  25.0 0.1 fusion.65
  25.1 0.7 convolution_bitcast_fusion.1
  25.8 4.7 %copy.70 = f32[4,128,128]{0,2,1:T(8,128)} copy(f32[4,128,128]{2,1,0:T(8,128)S(1)} %bitcast.107) | data formatting | bytes 524288 | tf_op jit(solution)/shard_map/squeeze | solution.py:59
  30.5 1.8 gather_fusion.3
  32.4 0.7 dynamic-slice_bitcast_fusion
  33.1 1.1 gather_fusion
  34.2 0.1 reshape.110
  34.4 1.1 gather_fusion.2
  35.5 0.1 reshape.124
  35.6 0.1 copy.66
  35.7 14.8 %all_gather.12 = bf16[16,128,128]{2,1,0:T(8,128)(2,1)S(1)} all-gather(bf16[4,128,128]{2,1,0:T(8,128)(2,1)S(1)} %copy.66), channel_id=1, replica_groups=mesh['job'=2,'seg'=4,'blk'=4] {'blk'}, dimensions={0}, use_global_device_ids=true | all-gather | bytes 655360 | tf_op jit(solution)/shard_map/all_gather | solution.py:65
  50.6 2.0 gather_fusion.1
  52.5 3.6 %multiply_reduce_fusion.3 = f32[4,128,128]{2,1,0:T(8,128)S(1)} fusion(bf16[1,4,12,128,128]{4,3,2,1,0:T(8,128)(2,1)S(1)} %copy-done, f32[4,12]{1,0:T(4,128)S(1)} %fusion.74, bf16[4,12,128,128]{3,2,1,0:T(8,128)(2,1)} %bitcast.109, bf16[1,4,12,128,128]{4,3,2,1,0:T(8,128)(2,1)} %param.13), kind=kOutput, calls=%fused_computation.12 | convolution fusion | flops 404946944 | bytes 4980928 | tf_op jit(solution)/shard_map/bkij,bkjl->bkil/dot_general | solution.py:74
  56.2 0.1 copy.69
  56.3 1.3 multiply_reduce_fusion.12
  57.6 9.5 %psum.71 = f32[]{:T(128)} all-reduce(f32[]{:T(128)} %get-tuple-element.24), channel_id=1, replica_groups=mesh['job'=2,'seg'=4,'blk'=4] {'blk'}, use_global_device_ids=true, to_apply=%region_4.5 | all-reduce | flops 1 | bytes 8 | tf_op jit(solution)/shard_map/psum | solution.py:94
  67.8 0.8 multiply_reduce_fusion.11
  68.7 10.6 %psum.72 = f32[]{:T(128)} all-reduce(f32[]{:T(128)} %get-tuple-element.18), channel_id=1, replica_groups=mesh['job'=2,'seg'=4,'blk'=4] {'blk'}, use_global_device_ids=true, to_apply=%region_6.7 | all-reduce | flops 1 | bytes 8 | tf_op jit(solution)/shard_map/psum | solution.py:81
  80.0 0.7 convolution_bitcast_fusion
  80.7 0.1 copy.76
  80.8 14.8 %all_gather.13 = bf16[16,128,128]{2,1,0:T(8,128)(2,1)S(1)} all-gather(bf16[4,128,128]{2,1,0:T(8,128)(2,1)S(1)} %copy.76), channel_id=1, replica_groups=mesh['job'=2,'seg'=4,'blk'=4] {'blk'}, dimensions={0}, use_global_device_ids=true | all-gather | bytes 655360 | tf_op jit(solution)/shard_map/all_gather | solution.py:65
  95.6 2.0 gather_fusion.5
  97.5 3.6 %multiply_reduce_fusion.2 = f32[4,128,128]{2,1,0:T(8,128)S(1)} fusion(bf16[1,4,12,128,128]{4,3,2,1,0:T(8,128)(2,1)S(1)} %copy-done, f32[4,12]{1,0:T(4,128)S(1)} %fusion.74, bf16[4,12,128,128]{3,2,1,0:T(8,128)(2,1)} %bitcast.110, bf16[1,4,12,128,128]{4,3,2,1,0:T(8,128)(2,1)} %param.13), kind=kOutput, calls=%fused_computation.11 | convolution fusion | flops 404946944 | bytes 4980928 | tf_op jit(solution)/shard_map/bkij,bkjl->bkil/dot_general | solution.py:74
  101.1 0.1 copy.79
  101.3 1.3 multiply_reduce_fusion.10
  102.5 9.6 %psum.73 = f32[]{:T(128)} all-reduce(f32[]{:T(128)} %get-tuple-element.26), channel_id=1, replica_groups=mesh['job'=2,'seg'=4,'blk'=4] {'blk'}, use_global_device_ids=true, to_apply=%region_9.10 | all-reduce | flops 1 | bytes 8 | tf_op jit(solution)/shard_map/psum | solution.py:94
  112.9 0.8 multiply_reduce_fusion.9
  113.7 10.4 %psum.74 = f32[]{:T(128)} all-reduce(f32[]{:T(128)} %get-tuple-element.16), channel_id=1, replica_groups=mesh['job'=2,'seg'=4,'blk'=4] {'blk'}, use_global_device_ids=true, to_apply=%region_11.12 | all-reduce | flops 1 | bytes 8 | tf_op jit(solution)/shard_map/psum | solution.py:81
  124.8 0.7 multiply_reduce_fusion.8
  125.5 0.7 fusion.47
  126.2 1.4 fusion.93
  127.6 1.5 collective-permute-start
  129.0 9.6 %psum.75 = f32[]{:T(128)} all-reduce(f32[]{:T(128)} %multiply_reduce_fusion.8), channel_id=1, replica_groups=mesh['job'=2,'seg'=4,'blk'=4] {'blk'}, use_global_device_ids=true, to_apply=%region_13.14 | all-reduce | flops 1 | bytes 8 | tf_op jit(solution)/shard_map/psum | solution.py:81
  139.4 0.1 fusion.68
  139.5 0.1 copy.85
  139.6 15.7 %all_gather.14 = bf16[16,128,128]{2,1,0:T(8,128)(2,1)S(1)} all-gather(bf16[4,128,128]{2,1,0:T(8,128)(2,1)S(1)} %copy.85), channel_id=1, replica_groups=mesh['job'=2,'seg'=4,'blk'=4] {'blk'}, dimensions={0}, use_global_device_ids=true | all-gather | bytes 655360 | tf_op jit(solution)/shard_map/all_gather | solution.py:65
  155.3 2.0 gather_fusion.6
  157.3 3.6 %multiply_reduce_fusion.1 = f32[4,128,128]{2,1,0:T(8,128)S(1)} fusion(bf16[1,4,12,128,128]{4,3,2,1,0:T(8,128)(2,1)S(1)} %copy-done, f32[4,12]{1,0:T(4,128)S(1)} %fusion.74, bf16[4,12,128,128]{3,2,1,0:T(8,128)(2,1)} %bitcast.111, bf16[1,4,12,128,128]{4,3,2,1,0:T(8,128)(2,1)} %param.13), kind=kOutput, calls=%fused_computation.10 | convolution fusion | flops 404946944 | bytes 4980928 | tf_op jit(solution)/shard_map/bkij,bkjl->bkil/dot_general | solution.py:74
  160.8 0.1 copy.88
  161.0 0.7 fusion.40
  161.7 4.7 %copy.89 = f32[4,128,128]{0,2,1:T(8,128)} copy(f32[4,128,128]{2,1,0:T(8,128)S(1)} %convert_add_fusion) | data formatting | bytes 524288 | tf_op jit(solution)/shard_map/add | solution.py:106
  166.4 1.8 gather_fusion.7
  168.2 1.4 multiply_reduce_fusion.7
  169.6 11.0 %psum.76 = f32[]{:T(128)} all-reduce(f32[]{:T(128)} %get-tuple-element.30), channel_id=1, replica_groups=mesh['job'=2,'seg'=4,'blk'=4] {'blk'}, use_global_device_ids=true, to_apply=%region_16.17 | all-reduce | flops 1 | bytes 8 | tf_op jit(solution)/shard_map/psum | solution.py:94
  181.2 0.8 multiply_reduce_fusion.6
  182.1 9.0 %psum.77 = f32[]{:T(128)} all-reduce(f32[]{:T(128)} %get-tuple-element.14), channel_id=1, replica_groups=mesh['job'=2,'seg'=4,'blk'=4] {'blk'}, use_global_device_ids=true, to_apply=%region_18.19 | all-reduce | flops 1 | bytes 8 | tf_op jit(solution)/shard_map/psum | solution.py:81
  191.8 0.6 fusion.44
  192.4 0.1 copy.96
  192.5 15.6 %all_gather.15 = bf16[16,128,128]{2,1,0:T(8,128)(2,1)S(1)} all-gather(bf16[4,128,128]{2,1,0:T(8,128)(2,1)S(1)} %copy.96), channel_id=1, replica_groups=mesh['job'=2,'seg'=4,'blk'=4] {'blk'}, dimensions={0}, use_global_device_ids=true | all-gather | bytes 655360 | tf_op jit(solution)/shard_map/all_gather | solution.py:65
  208.1 2.0 gather_fusion.8
  210.1 3.6 %multiply_reduce_fusion = f32[4,128,128]{2,1,0:T(8,128)S(1)} fusion(bf16[1,4,12,128,128]{4,3,2,1,0:T(8,128)(2,1)S(1)} %copy-done, f32[4,12]{1,0:T(4,128)S(1)} %fusion.74, bf16[4,12,128,128]{3,2,1,0:T(8,128)(2,1)} %bitcast.108, bf16[1,4,12,128,128]{4,3,2,1,0:T(8,128)(2,1)} %param.13), kind=kOutput, calls=%fused_computation.9 | convolution fusion | flops 404946944 | bytes 4980928 | tf_op jit(solution)/shard_map/bkij,bkjl->bkil/dot_general | solution.py:74
  213.6 0.1 copy.99
  213.8 1.3 multiply_reduce_fusion.5
  215.1 11.1 %psum.78 = f32[]{:T(128)} all-reduce(f32[]{:T(128)} %get-tuple-element.32), channel_id=1, replica_groups=mesh['job'=2,'seg'=4,'blk'=4] {'blk'}, use_global_device_ids=true, to_apply=%region_21.22 | all-reduce | flops 1 | bytes 8 | tf_op jit(solution)/shard_map/psum | solution.py:94
  226.8 0.8 multiply_reduce_fusion.4
  227.7 9.0 %psum.79 = f32[]{:T(128)} all-reduce(f32[]{:T(128)} %get-tuple-element.12), channel_id=1, replica_groups=mesh['job'=2,'seg'=4,'blk'=4] {'blk'}, use_global_device_ids=true, to_apply=%region_23.24 | all-reduce | flops 1 | bytes 8 | tf_op jit(solution)/shard_map/psum | solution.py:81
  237.4 0.8 copy.100
  238.2 0.6 maximum_bitcast_fusion
  (36 shorter events, 0.8 us)
Async XLA Ops:
  0.6 51.9 %copy-start = (bf16[1,4,12,128,128]{4,3,2,1,0:T(8,128)(2,1)S(1)}, bf16[1,4,12,128,128]{4,3,2,1,0:T(8,128)(2,1)}, u32[]{:S(2)}) copy-start(bf16[1,4,12,128,128]{4,3,2,1,0:T(8,128)(2,1)} %param.14) | copy-start | bytes 4718596
  1.5 5.8 %copy-start.4 = (f32[1,4,128,128]{3,2,1,0:T(8,128)S(1)}, f32[1,4,128,128]{3,2,1,0:T(8,128)}, u32[]{:S(2)}) copy-start(f32[1,4,128,128]{3,2,1,0:T(8,128)} %param.10) | copy-start | bytes 786436
  1.5 6.0 %copy-start.6 = (s32[4,2]{0,1:T(2,128)S(1)}, s32[4,2]{0,1:T(2,128)}, u32[]{:S(2)}) copy-start(s32[4,2]{0,1:T(2,128)} %param.16) | copy-start | bytes 100
  1.5 23.5 %copy-start.2 = (f32[1,4,128,128]{3,2,1,0:T(8,128)S(1)}, f32[1,4,128,128]{3,2,1,0:T(8,128)}, u32[]{:S(2)}) copy-start(f32[1,4,128,128]{3,2,1,0:T(8,128)} %param.11) | copy-start | bytes 786436
  25.8 6.5 %copy-start.5 = (s32[4,12]{1,0:T(4,128)S(1)}, s32[4,12]{1,0:T(4,128)}, u32[]{:S(2)}) copy-start(s32[4,12]{1,0:T(4,128)} %param.19) | copy-start | bytes 580
  30.5 3.9 %copy-start.1 = (s32[16,2]{0,1:T(2,128)S(1)}, s32[16,2]{0,1:T(2,128)}, u32[]{:S(2)}) copy-start(s32[16,2]{0,1:T(2,128)} %param.15) | copy-start | bytes 388
  52.5 3.8 %copy-start.3 = (f32[1,4,128,128]{3,2,1,0:T(8,128)S(1)}, f32[1,4,128,128]{3,2,1,0:T(8,128)}, u32[]{:S(2)}) copy-start(f32[1,4,128,128]{3,2,1,0:T(8,128)} %param.12) | copy-start | bytes 786436
  101.1 11.7 %copy-start.7 = (s32[4]{0:T(128)S(1)}, s32[4]{0:T(128)}, u32[]{:S(2)}) copy-start(s32[4]{0:T(128)} %param.17) | copy-start | bytes 52
  127.6 34.1 %collective-permute-start = (bf16[4,128,128]{2,1,0:T(8,128)(2,1)S(1)}, bf16[4,128,128]{2,1,0:T(8,128)(2,1)S(1)}, u32[]{:S(2)}, u32[]{:S(2)}) collective-permute-start(bf16[4,128,128]{2,1,0:T(8,128)(2,1)S(1)} %get-tuple-element.28), channel_id=1, source_target_pairs={{0,4},{4,8},{8,12},{1,5},{5,9},{9,13},{2,6},{6,10},{10,14},{3,7},{... | collective-permute-start | bytes 393224 | tf_op jit(solution)/shard_map/ppermute | solution.py:26
where the time goes:
time: 239 us
  blocking collectives  165 us (69%)
  local copies, waits for them, and re-layouts  34.6 us (14%)
  matrix products  24.3 us (10%)
  between operations  7.71 us (3%)
  other arithmetic  6.02 us (3%)
    psum x6, blocking collectives, global_squares(): return lax.psum(jnp.sum(values * values), 'blk')  62.7 us
    all_gather x4, blocking collectives, partners_of(): every_block = lax.all_gather(amp_half, 'blk', axis=0, tiled=True)  60.8 us
    psum x4, blocking collectives, davidson(): energy = lax.psum(jnp.sum(current * image), 'blk') / entries  41.2 us
    dot_general x4, matrix products, apply_ham(): jnp.einsum('bkij,bkjl->bkil', inner, hop_r, preferred_element_type=jnp.fl...  14.3 us
    gather x4, local copies, waits for them, and re-layouts, partners_of(): return every_block[partner]  7.81 us
    unnamed x19, local copies, waits for them, and re-layouts  6.8 us
    reduce_sum x6, other arithmetic, global_squares(): return lax.psum(jnp.sum(values * values), 'blk')  4.83 us
  transfers between devices with their start and end apart: 1, of which 0 were waited for; matrix products, arithmetic and copies ran while one was open for 3% of the time, Pallas kernels for 0%

commit v1 on v0

v1 whole, which is shorter than its diff:
```python
import functools

import jax
import jax.numpy as jnp
from jax import lax
from jax.experimental import pallas as pl
from jax.experimental.pallas import tpu as pltpu
from jax.sharding import PartitionSpec as P

ITERS = 2
STEP_SIZE = 0.5
ZEEMAN = 0.5
EPSILON = 1e-06
MESH = pl.DeviceIdType.MESH
F32 = jnp.float32
BF16 = jnp.bfloat16


def mm(a, b):
    return jnp.dot(a, b, preferred_element_type=F32)


def tile_sum(values):
    rows, cols = values.shape
    return jnp.sum(values.reshape(rows // 8, 8, cols), axis=0)


def split(values):
    high = values.astype(BF16)
    return high, (values - high.astype(F32)).astype(BF16)


def kernel(
    n, segs, nb, dim, nhop, cap,
    amp_hbm, left_hbm, right_hbm, hopl_hbm, hopr_hbm,
    charges, dims, kept, fetch, slots,
    wave_hbm, bound_hbm, energy_ref,
    t_v, left_v, right_v, hopl_v, hopr_v,
    signed, send, recv, lmat, rmat, tcol, trow, inner, local, field_diag, mask_v,
    parts, inc_v, inc_send, bound_v,
    in_sem, send_sem, recv_sem, psend_sem, precv_sem, isend_sem, irecv_sem, out_sem,
):
    me = lax.axis_index("blk")
    seg = lax.axis_index("seg")
    seg_next = lax.rem(seg + 1, segs)
    seg_prev = lax.rem(seg + segs - 1, segs)
    peers = [lax.rem(me + d, n) for d in range(1, n)]
    order = sorted(range(n - 1), key=lambda i: -min(i + 1, n - 1 - i))
    entries = float(n * nb * dim * dim)

    loads = [
        pltpu.make_async_copy(src.at[0], dst, in_sem.at[i])
        for i, (src, dst) in enumerate(
            [(amp_hbm, t_v), (left_hbm, left_v), (right_hbm, right_v), (hopl_hbm, hopl_v), (hopr_hbm, hopr_v)]
        )
    ]
    for load in loads:
        load.start()

    barrier = pltpu.get_barrier_semaphore()
    for peer in peers:
        pl.semaphore_signal(barrier, inc=1, device_id={"blk": peer}, device_id_type=MESH)
    pl.semaphore_signal(barrier, inc=1, device_id={"seg": seg_next}, device_id_type=MESH)
    pl.semaphore_signal(barrier, inc=1, device_id={"seg": seg_prev}, device_id_type=MESH)

    row_at = lax.broadcasted_iota(jnp.int32, (dim, dim), 0)
    col_at = lax.broadcasted_iota(jnp.int32, (dim, dim), 1)
    signs = [(1 - 2 * (charges[me * nb + b, 0] & 1)).astype(F32) for b in range(nb)]
    fields = [ZEEMAN * charges[me * nb + b, 1].astype(F32) for b in range(nb)]

    def block_copy(i):
        return pltpu.make_async_remote_copy(
            src_ref=send.at[pl.ds(i * cap, cap)],
            dst_ref=recv.at[pl.ds(me * cap, cap)],
            send_sem=send_sem.at[i],
            recv_sem=recv_sem.at[i],
            device_id={"blk": peers[i]},
            device_id_type=MESH,
        )

    def part_copy(turn, i):
        return pltpu.make_async_remote_copy(
            src_ref=parts.at[turn, me],
            dst_ref=parts.at[turn, me],
            send_sem=psend_sem.at[turn, i],
            recv_sem=precv_sem.at[turn, i],
            device_id={"blk": peers[i]},
            device_id_type=MESH,
        )

    def send_blocks():
        for i in order:
            for c in range(cap):
                send[i * cap + c] = signed[jnp.maximum(fetch[peers[i], me, c], 0)]
            block_copy(i).start()
        for c in range(cap):
            recv[me * cap + c] = signed[jnp.maximum(fetch[me, me, c], 0)]

    def wait_blocks():
        for i in range(n - 1):
            block_copy(i).wait()

    def send_parts(turn, squares, products):
        parts[turn, me] = jnp.concatenate([squares, products], axis=0)
        for i in order:
            part_copy(turn, i).start()

    def wait_parts(turn):
        for i in range(n - 1):
            part_copy(turn, i).wait()
        total = parts[turn, 0]
        for i in range(1, n):
            total = total + parts[turn, i]
        square = jnp.sum(total[0:8], axis=(0, 1), keepdims=True) / entries
        product = jnp.sum(total[8:16], axis=(0, 1), keepdims=True) / entries
        return square, product

    def split_t():
        for b in range(nb):
            high, low = split(t_v[b])
            tcol[b, 0:dim] = high
            tcol[b, dim:2 * dim] = high
            tcol[b, 2 * dim:3 * dim] = low
            trow[b, :, 0:dim] = high
            trow[b, :, dim:2 * dim] = high
            trow[b, :, 2 * dim:3 * dim] = low

    def set_left(b, value):
        high, low = split(value)
        lmat[b, :, 0:dim] = high
        lmat[b, :, dim:2 * dim] = low
        lmat[b, :, 2 * dim:3 * dim] = high

    def diag_column(value):
        return jnp.sum(jnp.where(row_at == col_at, value, 0.0), axis=1, keepdims=True)

    def diag_row(value):
        return jnp.sum(jnp.where(row_at == col_at, value, 0.0), axis=0, keepdims=True)

    def hopping():
        products = jnp.zeros((8, dim), F32)
        for b in range(nb):
            for k in range(nhop):
                inner[b, :, k * dim:(k + 1) * dim] = mm(hopl_v[b, k], recv[slots[b, k]]).astype(BF16)
            image = local[b] + mm(inner[b], hopr_v[b].reshape(nhop * dim, dim))
            local[b] = image
            products = products + tile_sum(t_v[b] * image)
        return products

    def step(energy, scale):
        squares = jnp.zeros((8, dim), F32)
        for b in range(nb):
            old = t_v[b]
            change = mask_v[b] * (local[b] - energy * old) / (1.0 + jnp.abs(field_diag[b] - energy))
            new = scale * (old - STEP_SIZE * change)
            t_v[b] = new
            signed[b] = (new * signs[b]).astype(BF16)
            squares = squares + tile_sum(new * new)
        return squares

    squares = jnp.zeros((8, dim), F32)
    loads[0].wait()
    for b in range(nb):
        live = jnp.where((row_at < dims[b, 0]) & (col_at < dims[b, 1]), 1.0, 0.0)
        mask_v[b] = live
        new = live * t_v[b]
        t_v[b] = new
        signed[b] = (new * signs[b]).astype(BF16)
        squares = squares + tile_sum(new * new)
    pl.semaphore_wait(barrier, n + 1)

    zeros = jnp.zeros((8, dim), F32)
    turn = 0
    energies = []
    for update in range(2):
        for iteration in range(ITERS):
            send_blocks()
            if update == 1 and iteration == 0:
                send_parts(turn, squares, zeros)
            split_t()
            if update == 0 and iteration == 0:
                loads[1].wait()
                loads[2].wait()
                for b in range(nb):
                    set_left(b, left_v[b])
                    high, low = split(right_v[b])
                    rmat[b, 0:dim] = high
                    rmat[b, dim:2 * dim] = low
                    rmat[b, 2 * dim:3 * dim] = high
                    field_diag[b] = diag_column(left_v[b]) + diag_row(right_v[b]) + fields[b]
            if update == 1 and iteration == 0:
                for b in range(nb):
                    from_left = mm(lmat[b], tcol[b])
                    local[b] = from_left + mm(trow[b], rmat[b]) + fields[b] * t_v[b]
                    high, low = split(from_left)
                    bound_v[b] = lax.dot_general(
                        tcol[b],
                        jnp.concatenate([high, low, high], axis=0),
                        (((0,), (0,)), ((), ())),
                        preferred_element_type=F32,
                    )
                square, _ = wait_parts(turn)
                turn = 1 - turn
                scale = lax.rsqrt(square + EPSILON)
                for b in range(nb):
                    keep = (row_at < kept[b]) & (col_at < kept[b])
                    outgoing = jnp.where(keep, bound_v[b] * (scale * scale * (1.0 / dim)), 0.0)
                    bound_v[b] = outgoing
                    inc_send[b] = outgoing.astype(BF16)
                inc_copy = pltpu.make_async_remote_copy(
                    src_ref=inc_send,
                    dst_ref=inc_v,
                    send_sem=isend_sem,
                    recv_sem=irecv_sem,
                    device_id={"seg": seg_next},
                    device_id_type=MESH,
                )
                inc_copy.start()
                bound_out = pltpu.make_async_copy(bound_v, bound_hbm.at[0], out_sem.at[0])
                bound_out.start()
                inc_copy.wait()
                for b in range(nb):
                    incoming = jnp.where(seg > 0, inc_v[b], jnp.zeros((dim, dim), BF16))
                    wide = incoming.astype(F32)
                    local[b] = local[b] + mm(
                        jnp.concatenate([incoming, incoming], axis=1), tcol[b, dim:3 * dim]
                    )
                    set_left(b, left_v[b] + wide)
                    field_diag[b] = field_diag[b] + diag_column(wide)
            else:
                for b in range(nb):
                    local[b] = mm(lmat[b], tcol[b]) + mm(trow[b], rmat[b]) + fields[b] * t_v[b]
            if update == 0 and iteration == 0:
                loads[3].wait()
                loads[4].wait()
            wait_blocks()
            products = hopping()
            send_parts(turn, squares, products)
            square, product = wait_parts(turn)
            turn = 1 - turn
            scale = lax.rsqrt(square + EPSILON)
            if update == 1 and iteration == 0:
                scale = scale * lax.rsqrt(square * scale * scale + EPSILON)
            energy = product * scale * scale
            squares = step(energy, scale)
        energies.append(energy)

    send_parts(turn, squares, zeros)
    which = lax.broadcasted_iota(jnp.int32, (1, 2), 1)
    energy_ref[...] = jnp.where(which == 0, energies[0], energies[1])
    square, _ = wait_parts(turn)
    scale = lax.rsqrt(square + EPSILON)
    for b in range(nb):
        t_v[b] = t_v[b] * scale
    wave_out = pltpu.make_async_copy(t_v, wave_hbm.at[0], out_sem.at[1])
    wave_out.start()
    bound_out.wait()
    wave_out.wait()


def on_device(n, segs, *args):
    amplitudes, left_env, right_env, hop_left, hop_right, charges, dims, kept, fetch, slots = args
    nb, dim = amplitudes.shape[1], amplitudes.shape[2]
    nhop = hop_left.shape[2]
    cap = fetch.shape[2]
    any_space = pl.BlockSpec(memory_space=pl.ANY)
    smem = pl.BlockSpec(memory_space=pltpu.SMEM)
    vmem = pl.BlockSpec(memory_space=pltpu.VMEM)
    blocks = (nb, dim, dim)
    dma = pltpu.SemaphoreType.DMA
    scratch = [
        pltpu.VMEM(blocks, F32),
        pltpu.VMEM(blocks, F32),
        pltpu.VMEM(blocks, F32),
        pltpu.VMEM((nb, nhop, dim, dim), BF16),
        pltpu.VMEM((nb, nhop, dim, dim), BF16),
        pltpu.VMEM(blocks, BF16),
        pltpu.VMEM(((n - 1) * cap, dim, dim), BF16),
        pltpu.VMEM((n * cap, dim, dim), BF16),
        pltpu.VMEM((nb, dim, 3 * dim), BF16),
        pltpu.VMEM((nb, 3 * dim, dim), BF16),
        pltpu.VMEM((nb, 3 * dim, dim), BF16),
        pltpu.VMEM((nb, dim, 3 * dim), BF16),
        pltpu.VMEM((nb, dim, nhop * dim), BF16),
        pltpu.VMEM(blocks, F32),
        pltpu.VMEM(blocks, F32),
        pltpu.VMEM(blocks, F32),
        pltpu.VMEM((2, n, 16, dim), F32),
        pltpu.VMEM(blocks, BF16),
        pltpu.VMEM(blocks, BF16),
        pltpu.VMEM(blocks, F32),
        dma((5,)),
        dma((n - 1,)),
        dma((n - 1,)),
        dma((2, n - 1)),
        dma((2, n - 1)),
        dma,
        dma,
        dma((2,)),
    ]
    return pl.pallas_call(
        functools.partial(kernel, n, segs, nb, dim, nhop, cap),
        out_shape=(
            jax.ShapeDtypeStruct(amplitudes.shape, F32),
            jax.ShapeDtypeStruct(amplitudes.shape, F32),
            jax.ShapeDtypeStruct((1, 2), F32),
        ),
        in_specs=[any_space] * 5 + [smem] * 5,
        out_specs=(any_space, any_space, vmem),
        scratch_shapes=scratch,
        compiler_params=pltpu.CompilerParams(
            collective_id=0, has_side_effects=True, vmem_limit_bytes=40 * 1024 * 1024
        ),
    )(amplitudes, left_env, right_env, hop_left, hop_right, charges, dims, kept, fetch, slots)


def solution(mesh):
    placed = (
        P(("job", "seg"), "blk", None, None),
        P(("job", "seg"), "blk", None, None),
        P(("job", "seg"), "blk", None, None),
        P(("job", "seg"), "blk", None, None, None),
        P(("job", "seg"), "blk", None, None, None),
        P("job", None),
        P(("job", "blk"), None),
        P(("job", "blk")),
        P("job", None, None),
        P(("job", "blk"), None),
    )
    return jax.shard_map(
        functools.partial(on_device, mesh.shape["blk"], mesh.shape["seg"]),
        mesh=mesh,
        in_specs=placed,
        out_specs=(
            P(("job", "seg"), "blk", None, None),
            P(("job", "seg"), "blk", None, None),
            P(("job", "seg"), None),
        ),
        check_vma=False,
    )
```

time: 239 us -> 69 us (0.29)
  blocking collectives: 165 us -> 0 us
  Pallas kernels: 0 us -> 56.7 us
  matrix products: 24.3 us -> 0 us
  local copies, waits for them, and re-layouts: 34.6 us -> 11.2 us
  between operations: 7.71 us -> 0.65 us
  other arithmetic: 6.02 us -> 0 us
    psum x10 -> x0, blocking collectives: 104 us -> none  [the longest x6 62.7 us: global_squares(): return lax.psum(jnp.sum(values * values), 'blk')]
    all_gather x4 -> x0, blocking collectives: 60.8 us -> none  [partners_of(): every_block = lax.all_gather(amp_half, 'blk', axis=0, tiled=True)]
    pallas_call x0 -> x1, Pallas kernels: none -> 56.7 us  [on_device(): pl.pallas_call(functools.partial(kernel, n, segs, nb, dim, nhop, cap), ou...]
    dot_general x14 -> x0, matrix products: 24.3 us -> none  [the longest x4 14.3 us: apply_ham(): jnp.einsum('bkij,bkjl->bkil', inner, hop_r, preferred_element_type=jnp.fl...]
    gather x14 -> x0, local copies, waits for them, and re-layouts: 15.6 us -> none  [the longest x4 7.81 us: partners_of(): return every_block[partner]]
    squeeze x2 -> x0, local copies, waits for them, and re-layouts: 5.35 us -> none  [the longest x1 4.67 us: on_device(): left_own = left_env[0]]
    reduce_sum x6 -> x0, other arithmetic: 4.83 us -> none  [global_squares(): return lax.psum(jnp.sum(values * values), 'blk')]
    add x1 -> x0, local copies, waits for them, and re-layouts: 4.67 us -> none  [on_device(): final_wave, second_energy = davidson(updated, left_own + incoming)]
  transfers between devices with their start and end apart: 1 -> 0, of which waited for: 0 -> 0; matrix products, arithmetic and copies ran while one was open for 3% -> 0% of each run, Pallas kernels for 0% -> 0%
where the time goes in v1:
time: 69 us; the launch traced here: 68.6 us
  Pallas kernels  56.7 us (82%)
  local copies, waits for them, and re-layouts  11.2 us (16%)
    pallas_call x1, Pallas kernels, on_device(): pl.pallas_call(functools.partial(kernel, n, segs, nb, dim, nhop, cap), ou...  56.7 us
    unnamed x20, local copies, waits for them, and re-layouts  11.2 us

profile of v1, /device:TPU:0, one launch (start us, length us, event | category | flops | bytes accessed | tf_op | source)
XLA Modules:
  0.0 68.6 jit_solution(3487544152670676664)
XLA Ops:
  0.6 0.8 %copy.14.dims = s32[4,2]{1,0:T(4,128)S(1)} copy(s32[4,2]{0,1:T(2,128)} %param.16) | data formatting | bytes 64 | tf_op args[6]
  1.4 0.8 %copy.13.charges = s32[16,2]{1,0:T(8,128)S(1)} copy(s32[16,2]{0,1:T(2,128)} %param.15) | data formatting | bytes 256 | tf_op args[5]
  2.2 0.8 %copy.15.fetch = s32[4,4,2]{2,1,0:T(4,128)S(1)} copy(s32[4,4,2]{1,2,0:T(2,128)} %param.18) | data formatting | bytes 256 | tf_op args[8]
  2.9 0.0 copy-start
  2.9 1.4 %copy-done = bf16[1,4,12,128,128]{4,3,2,1,0:T(8,128)(2,1)S(1)} copy-done((bf16[1,4,12,128,128]{4,3,2,1,0:T(8,128)(2,1)S(1)}, bf16[1,4,12,128,128]{4,3,2,1,0:T(8,128)(2,1)}, u32[]{:S(2)}) %copy-start) | copy-done | bytes 1572888
  4.3 0.0 copy-start.1
  4.4 1.4 %copy-done.1 = bf16[1,4,12,128,128]{4,3,2,1,0:T(8,128)(2,1)S(1)} copy-done((bf16[1,4,12,128,128]{4,3,2,1,0:T(8,128)(2,1)S(1)}, bf16[1,4,12,128,128]{4,3,2,1,0:T(8,128)(2,1)}, u32[]{:S(2)}) %copy-start.1) | copy-done | bytes 1572888
  5.8 0.0 copy-start.2
  5.8 0.9 %copy-done.2 = f32[1,4,128,128]{3,2,1,0:T(8,128)S(1)} copy-done((f32[1,4,128,128]{3,2,1,0:T(8,128)S(1)}, f32[1,4,128,128]{3,2,1,0:T(8,128)}, u32[]{:S(2)}) %copy-start.2) | copy-done | bytes 262168
  6.7 0.0 copy-start.3
  6.7 0.9 %copy-done.3 = f32[1,4,128,128]{3,2,1,0:T(8,128)S(1)} copy-done((f32[1,4,128,128]{3,2,1,0:T(8,128)S(1)}, f32[1,4,128,128]{3,2,1,0:T(8,128)}, u32[]{:S(2)}) %copy-start.3) | copy-done | bytes 262168
  7.7 0.0 copy-start.4
  7.7 0.9 %copy-done.4 = f32[1,4,128,128]{3,2,1,0:T(8,128)S(1)} copy-done((f32[1,4,128,128]{3,2,1,0:T(8,128)S(1)}, f32[1,4,128,128]{3,2,1,0:T(8,128)}, u32[]{:S(2)}) %copy-start.4) | copy-done | bytes 262168
  8.6 0.0 copy-start.5
  8.6 0.7 copy-done.5
  9.3 0.0 copy-start.6
  9.3 0.7 copy-done.6
  9.9 56.7 %shard_map.121 = (f32[1,4,128,128]{3,2,1,0:T(8,128)S(1)}, f32[1,4,128,128]{3,2,1,0:T(8,128)S(1)}, f32[1,2]{1,0:T(1,128)S(1)}) custom-call(f32[1,4,128,128]{3,2,1,0:T(8,128)S(1)} %copy-done.2, f32[1,4,128,128]{3,2,1,0:T(8,128)S(1)} %copy-done.3, f32[1,4,128,128]{3,2,1,0:T(8,128)S(1)} %copy-done.4, bf16[1,4,12,128,128]{4,3,2,1,0:T(8,128)(2,1)S(1)} %copy-done, ...), custom_call_target="tpu_custom_call" | custom-call | tf_op jit(solution)/shard_map/pallas_call | solution.py:301
  66.7 0.7 %copy.19 = f32[1,4,128,128]{3,2,1,0:T(8,128)} copy(f32[1,4,128,128]{3,2,1,0:T(8,128)S(1)} %get-tuple-element.6) | data formatting | bytes 524288
  67.4 0.7 %copy.20 = f32[1,4,128,128]{3,2,1,0:T(8,128)} copy(f32[1,4,128,128]{3,2,1,0:T(8,128)S(1)} %get-tuple-element.7) | data formatting | bytes 524288
  68.1 0.5 copy.21
Async XLA Ops:
  2.9 1.4 %copy-start = (bf16[1,4,12,128,128]{4,3,2,1,0:T(8,128)(2,1)S(1)}, bf16[1,4,12,128,128]{4,3,2,1,0:T(8,128)(2,1)}, u32[]{:S(2)}) copy-start(bf16[1,4,12,128,128]{4,3,2,1,0:T(8,128)(2,1)} %hopl_hbm.1) | copy-start | bytes 4718596
  4.3 1.4 %copy-start.1 = (bf16[1,4,12,128,128]{4,3,2,1,0:T(8,128)(2,1)S(1)}, bf16[1,4,12,128,128]{4,3,2,1,0:T(8,128)(2,1)}, u32[]{:S(2)}) copy-start(bf16[1,4,12,128,128]{4,3,2,1,0:T(8,128)(2,1)} %hopr_hbm.1) | copy-start | bytes 4718596
  5.8 0.9 %copy-start.2 = (f32[1,4,128,128]{3,2,1,0:T(8,128)S(1)}, f32[1,4,128,128]{3,2,1,0:T(8,128)}, u32[]{:S(2)}) copy-start(f32[1,4,128,128]{3,2,1,0:T(8,128)} %amp_hbm.1) | copy-start | bytes 786436
  6.7 0.9 %copy-start.3 = (f32[1,4,128,128]{3,2,1,0:T(8,128)S(1)}, f32[1,4,128,128]{3,2,1,0:T(8,128)}, u32[]{:S(2)}) copy-start(f32[1,4,128,128]{3,2,1,0:T(8,128)} %left_hbm.1) | copy-start | bytes 786436
  7.7 0.9 %copy-start.4 = (f32[1,4,128,128]{3,2,1,0:T(8,128)S(1)}, f32[1,4,128,128]{3,2,1,0:T(8,128)}, u32[]{:S(2)}) copy-start(f32[1,4,128,128]{3,2,1,0:T(8,128)} %right_hbm.1) | copy-start | bytes 786436
  8.6 0.7 copy-start.5
  9.3 0.7 copy-start.6

commit v2 on v1

v2 whole, which is shorter than its diff:
```python
import functools

import jax
import jax.numpy as jnp
from jax import lax
from jax.experimental import pallas as pl
from jax.experimental.pallas import tpu as pltpu
from jax.sharding import PartitionSpec as P

ITERS = 2
STEP_SIZE = 0.5
ZEEMAN = 0.5
EPSILON = 1e-06
MESH = pl.DeviceIdType.MESH
F32 = jnp.float32
BF16 = jnp.bfloat16


def mm(a, b):
    return jnp.dot(a, b, preferred_element_type=F32)


def tile_sum(values):
    rows, cols = values.shape
    return jnp.sum(values.reshape(rows // 8, 8, cols), axis=0)


def split(values):
    high = values.astype(BF16)
    return high, (values - high.astype(F32)).astype(BF16)


def each(count, body):
    if count <= 16:
        for index in range(count):
            body(index)
    else:
        lax.fori_loop(0, count, lambda index, _: (body(index), 0)[1], 0)


def kernel(
    n, segs, nb, dim, nhop, cap,
    amp_hbm, left_hbm, right_hbm, hopl_hbm, hopr_hbm,
    charges, dims, kept, fetch, slots,
    wave_hbm, bound_hbm, energy_ref,
    t_v, left_v, right_v, hopl_v, hopr_v,
    signed, send, recv, lmat, rmat, tcol, trow, inner, local, diag_v, mask_v,
    parts, inc_v, inc_send, bound_v,
    copy_v, slot_t, slot_x, slot_diag, vec_v, vec_send, vec_recv, norm_send, norm_recv,
    in_sem, send_sem, recv_sem, psend_sem, precv_sem, isend_sem, irecv_sem, out_sem,
    vsend_sem, vrecv_sem, nsend_sem, nrecv_sem,
):
    me = lax.axis_index("blk")
    seg = lax.axis_index("seg")
    seg_next = lax.rem(seg + 1, segs)
    seg_prev = lax.rem(seg + segs - 1, segs)
    peers = [lax.rem(me + d, n) for d in range(1, n)]
    group = [lax.rem(me + d, n) for d in range(n)]
    order = sorted(range(n - 1), key=lambda i: -min(i + 1, n - 1 - i))
    entries = float(n * nb * dim * dim)

    loads = [
        pltpu.make_async_copy(src.at[0], dst, in_sem.at[i])
        for i, (src, dst) in enumerate(
            [(amp_hbm, t_v), (left_hbm, left_v), (right_hbm, right_v), (hopl_hbm, hopl_v), (hopr_hbm, hopr_v)]
        )
    ]
    for load in loads:
        load.start()

    barrier = pltpu.get_barrier_semaphore()
    for peer in peers:
        pl.semaphore_signal(barrier, inc=1, device_id={"blk": peer}, device_id_type=MESH)
    for peer in group:
        for other in (seg_next, seg_prev):
            pl.semaphore_signal(barrier, inc=1, device_id={"seg": other, "blk": peer}, device_id_type=MESH)

    row_at = lax.broadcasted_iota(jnp.int32, (dim, dim), 0)
    col_at = lax.broadcasted_iota(jnp.int32, (dim, dim), 1)
    signs = [(1 - 2 * (charges[0, me * nb + b] & 1)).astype(F32) for b in range(nb)]
    fields = [ZEEMAN * charges[1, me * nb + b].astype(F32) for b in range(nb)]

    def block_copy(half, i):
        return pltpu.make_async_remote_copy(
            src_ref=send.at[pl.ds(i * cap, cap)],
            dst_ref=recv.at[half, pl.ds(me * cap, cap)],
            send_sem=send_sem.at[half, i],
            recv_sem=recv_sem.at[half, i],
            device_id={"blk": peers[i]},
            device_id_type=MESH,
        )

    def part_copy(turn, i):
        return pltpu.make_async_remote_copy(
            src_ref=parts.at[turn, me],
            dst_ref=parts.at[turn, me],
            send_sem=psend_sem.at[turn, i],
            recv_sem=precv_sem.at[turn, i],
            device_id={"blk": peers[i]},
            device_id_type=MESH,
        )

    def vec_copy(i):
        return pltpu.make_async_remote_copy(
            src_ref=vec_send.at[pl.ds(i * cap, cap)],
            dst_ref=vec_recv.at[pl.ds(me * cap, cap)],
            send_sem=vsend_sem.at[i],
            recv_sem=vrecv_sem.at[i],
            device_id={"blk": peers[i]},
            device_id_type=MESH,
        )

    def norm_copy(i):
        return pltpu.make_async_remote_copy(
            src_ref=norm_send,
            dst_ref=norm_recv.at[me],
            send_sem=nsend_sem.at[i],
            recv_sem=nrecv_sem.at[i],
            device_id={"blk": group[i], "seg": seg_next},
            device_id_type=MESH,
        )

    def picked(device, c):
        return jnp.maximum(fetch[device, c, me], 0)

    def send_blocks(half):
        for i in order:
            for c in range(cap):
                send[i * cap + c] = signed[picked(peers[i], c)]
            block_copy(half, i).start()
        for c in range(cap):
            recv[half, me * cap + c] = signed[picked(me, c)]

    def wait_blocks(half):
        for i in range(n - 1):
            block_copy(half, i).wait()

    def diag_row(value):
        return jnp.sum(jnp.where(row_at == col_at, value, 0.0), axis=0, keepdims=True)

    def diag_of(pair):
        column = jnp.sum(jnp.where(row_at == col_at, pair[0:1], 0.0), axis=1, keepdims=True)
        return column + pair[1:2]

    def send_vecs():
        for i in order:
            for c in range(cap):
                vec_send[i * cap + c] = vec_v[picked(peers[i], c)]
            vec_copy(i).start()
        for c in range(cap):
            vec_recv[me * cap + c] = vec_v[picked(me, c)]

    def wait_vecs():
        for i in range(n - 1):
            vec_copy(i).wait()

        def one(index):
            slot_diag[index] = diag_of(vec_recv[index])

        each(n * cap, one)

    def send_parts(turn, squares, products):
        parts[turn, me] = jnp.concatenate([squares, products], axis=0)
        for i in order:
            part_copy(turn, i).start()

    def total_of(tile):
        return jnp.sum(tile, axis=(0, 1), keepdims=True)

    def wait_parts(turn):
        for i in range(n - 1):
            part_copy(turn, i).wait()
        total = parts[turn, 0]
        for i in range(1, n):
            total = total + parts[turn, i]
        return total_of(total[0:8]) / entries, total_of(total[8:16]) / entries

    def split_t():
        for b in range(nb):
            high, low = split(t_v[b])
            tcol[b, 0:dim] = high
            tcol[b, dim:2 * dim] = high
            tcol[b, 2 * dim:3 * dim] = low
            trow[b, :, 0:dim] = high
            trow[b, :, dim:2 * dim] = high
            trow[b, :, 2 * dim:3 * dim] = low

    def set_left(b, value):
        high, low = split(value)
        lmat[b, :, 0:dim] = high
        lmat[b, :, dim:2 * dim] = low
        lmat[b, :, 2 * dim:3 * dim] = high

    def local_products(with_left):
        for b in range(nb):
            value = mm(trow[b], rmat[b]) + fields[b] * t_v[b]
            if with_left:
                value = value + mm(lmat[b], tcol[b])
            local[b] = value

    def hopping(finish):
        for b in range(nb):
            for k in range(nhop):
                inner[b, :, k * dim:(k + 1) * dim] = mm(hopl_v[b, k], slot_x[slots[b, k]]).astype(BF16)
            local[b] = local[b] + mm(inner[b], hopr_v[b].reshape(nhop * dim, dim))
        finish()
        products = jnp.zeros((8, dim), F32)
        for b in range(nb):
            image = mask_v[b] * local[b]
            local[b] = image
            products = products + tile_sum(t_v[b] * image)
        return products

    def send_image(half, squares, products):
        guess = total_of(products) / (total_of(squares) + 1e-30)
        for b in range(nb):
            behind = signs[b] * t_v[b] - copy_v[b]
            weight = guess + (1.0 / STEP_SIZE) * (1.0 + jnp.abs(diag_v[b] - guess))
            signed[b] = (signs[b] * local[b] - behind * weight).astype(BF16)
        send_blocks(half)

    def advance(old, image, diag, energy, scale):
        change = (image - energy * old) / (1.0 + jnp.abs(diag - energy))
        return scale * (old - STEP_SIZE * change)

    def step(energy, scale):
        squares = jnp.zeros((8, dim), F32)
        for b in range(nb):
            new = advance(t_v[b], local[b], diag_v[b], energy, scale)
            t_v[b] = new
            squares = squares + tile_sum(new * new)
        return squares

    def step_copies(energy, scale):
        for b in range(nb):
            copy_v[b] = advance(copy_v[b], signed[b].astype(F32), diag_v[b], energy, scale)

    def step_slots(half, energy, scale):
        def one(index):
            new = advance(slot_t[index], recv[half, index].astype(F32), slot_diag[index], energy, scale)
            slot_t[index] = new
            slot_x[index] = new.astype(BF16)

        each(n * cap, one)

    def nothing():
        pass

    squares = jnp.zeros((8, dim), F32)
    loads[0].wait()
    for b in range(nb):
        live = jnp.where((row_at < dims[0, b]) & (col_at < dims[1, b]), 1.0, 0.0)
        mask_v[b] = live
        new = live * t_v[b]
        t_v[b] = new
        first = (new * signs[b]).astype(BF16)
        signed[b] = first
        copy_v[b] = first.astype(F32)
        squares = squares + tile_sum(new * new)
    pl.semaphore_wait(barrier, n - 1 + 2 * n)
    send_blocks(0)
    loads[1].wait()
    loads[2].wait()
    for b in range(nb):
        vec_v[b, 0:1] = diag_row(left_v[b]) + fields[b]
        vec_v[b, 1:2] = diag_row(right_v[b])
    send_vecs()
    split_t()
    for b in range(nb):
        set_left(b, left_v[b])
        high, low = split(right_v[b])
        rmat[b, 0:dim] = high
        rmat[b, dim:2 * dim] = low
        rmat[b, 2 * dim:3 * dim] = high
        diag_v[b] = diag_of(vec_v[b])
    local_products(True)
    loads[3].wait()
    loads[4].wait()
    wait_blocks(0)

    def widen(index):
        first = recv[0, index]
        slot_x[index] = first
        slot_t[index] = first.astype(F32)

    each(n * cap, widen)

    products = hopping(nothing)
    send_parts(0, squares, products)
    send_image(1, squares, products)
    wait_vecs()
    square, product = wait_parts(0)
    scale = lax.rsqrt(square + EPSILON)
    energy = product * scale * scale
    squares = step(energy, scale)
    step_copies(energy, scale)
    split_t()
    local_products(True)
    wait_blocks(1)
    step_slots(1, energy, scale)

    products = hopping(nothing)
    send_parts(1, squares, products)
    send_image(0, squares, products)
    square, product = wait_parts(1)
    scale = lax.rsqrt(square + EPSILON)
    energy = product * scale * scale
    first_energy = energy
    squares = step(energy, scale)
    norm_send[...] = squares
    for i in range(n):
        norm_copy(i).start()
    split_t()
    for b in range(nb):
        high, low = split(mm(lmat[b], tcol[b]))
        raw = lax.dot_general(
            tcol[b],
            jnp.concatenate([high, low, high], axis=0),
            (((0,), (0,)), ((), ())),
            preferred_element_type=F32,
        )
        keep = (row_at < kept[b]) & (col_at < kept[b])
        raw = jnp.where(keep, raw, 0.0)
        bound_v[b] = raw
        inc_send[b] = raw.astype(BF16)
    inc_copy = pltpu.make_async_remote_copy(
        src_ref=inc_send,
        dst_ref=inc_v,
        send_sem=isend_sem,
        recv_sem=irecv_sem,
        device_id={"seg": seg_next},
        device_id_type=MESH,
    )
    inc_copy.start()
    step_copies(energy, scale)
    local_products(False)
    wait_blocks(0)
    step_slots(0, energy, scale)

    def add_left():
        for i in range(n):
            norm_copy(i).wait()
        total = norm_recv[0]
        for i in range(1, n):
            total = total + norm_recv[i]
        factor = (1.0 / dim) / (total_of(total) / entries + EPSILON)
        factor = jnp.where(seg > 0, factor, 0.0)
        inc_copy.wait()
        for b in range(nb):
            wide = inc_v[b].astype(F32) * factor
            set_left(b, left_v[b] + wide)
            local[b] = local[b] + mm(lmat[b], tcol[b])
            vec_v[b, 0:1] = vec_v[b, 0:1] + diag_row(wide)
            diag_v[b] = diag_of(vec_v[b])

    products = hopping(add_left)
    send_parts(0, squares, products)
    send_image(1, squares, products)
    send_vecs()
    square, product = wait_parts(0)
    scale = lax.rsqrt(square + EPSILON)
    factor = scale * scale * (1.0 / dim)
    scale = scale * lax.rsqrt(square * scale * scale + EPSILON)
    energy = product * scale * scale
    squares = step(energy, scale)
    split_t()
    local_products(True)
    for b in range(nb):
        bound_v[b] = bound_v[b] * factor
    bound_out = pltpu.make_async_copy(bound_v, bound_hbm.at[0], out_sem.at[0])
    bound_out.start()
    wait_vecs()
    wait_blocks(1)
    step_slots(1, energy, scale)

    products = hopping(nothing)
    send_parts(1, squares, products)
    square, product = wait_parts(1)
    scale = lax.rsqrt(square + EPSILON)
    energy = product * scale * scale
    squares = step(energy, scale)
    send_parts(0, squares, jnp.zeros((8, dim), F32))
    which = lax.broadcasted_iota(jnp.int32, (1, 2), 1)
    energy_ref[...] = jnp.where(which == 0, first_energy, energy)
    square, _ = wait_parts(0)
    scale = lax.rsqrt(square + EPSILON)
    for b in range(nb):
        t_v[b] = t_v[b] * scale
    wave_out = pltpu.make_async_copy(t_v, wave_hbm.at[0], out_sem.at[1])
    wave_out.start()
    bound_out.wait()
    wave_out.wait()


def finish(wave, bound, energy, wave_hbm, bound_hbm, energy_hbm, sems):
    copies = [
        pltpu.make_async_copy(src, dst, sems.at[i])
        for i, (src, dst) in enumerate([(wave, wave_hbm), (bound, bound_hbm), (energy, energy_hbm)])
    ]
    for copy in copies:
        copy.start()
    for copy in copies:
        copy.wait()


def on_device(n, segs, *args):
    amplitudes, left_env, right_env, hop_left, hop_right, charges, dims, kept, fetch, slots = args
    nb, dim = amplitudes.shape[1], amplitudes.shape[2]
    nhop = hop_left.shape[2]
    cap = fetch.shape[2]
    any_space = pl.BlockSpec(memory_space=pl.ANY)
    hbm = pl.BlockSpec(memory_space=pltpu.HBM)
    smem = pl.BlockSpec(memory_space=pltpu.SMEM)
    vmem = pl.BlockSpec(memory_space=pltpu.VMEM)
    blocks = (nb, dim, dim)
    dma = pltpu.SemaphoreType.DMA
    scratch = [
        pltpu.VMEM(blocks, F32),
        pltpu.VMEM(blocks, F32),
        pltpu.VMEM(blocks, F32),
        pltpu.VMEM((nb, nhop, dim, dim), BF16),
        pltpu.VMEM((nb, nhop, dim, dim), BF16),
        pltpu.VMEM(blocks, BF16),
        pltpu.VMEM(((n - 1) * cap, dim, dim), BF16),
        pltpu.VMEM((2, n * cap, dim, dim), BF16),
        pltpu.VMEM((nb, dim, 3 * dim), BF16),
        pltpu.VMEM((nb, 3 * dim, dim), BF16),
        pltpu.VMEM((nb, 3 * dim, dim), BF16),
        pltpu.VMEM((nb, dim, 3 * dim), BF16),
        pltpu.VMEM((nb, dim, nhop * dim), BF16),
        pltpu.VMEM(blocks, F32),
        pltpu.VMEM(blocks, F32),
        pltpu.VMEM(blocks, F32),
        pltpu.VMEM((2, n, 16, dim), F32),
        pltpu.VMEM(blocks, BF16),
        pltpu.VMEM(blocks, BF16),
        pltpu.VMEM(blocks, F32),
        pltpu.VMEM(blocks, F32),
        pltpu.VMEM((n * cap, dim, dim), F32),
        pltpu.VMEM((n * cap, dim, dim), BF16),
        pltpu.VMEM((n * cap, dim, dim), F32),
        pltpu.VMEM((nb, 8, dim), F32),
        pltpu.VMEM(((n - 1) * cap, 8, dim), F32),
        pltpu.VMEM((n * cap, 8, dim), F32),
        pltpu.VMEM((8, dim), F32),
        pltpu.VMEM((n, 8, dim), F32),
        dma((5,)),
        dma((2, n - 1)),
        dma((2, n - 1)),
        dma((2, n - 1)),
        dma((2, n - 1)),
        dma,
        dma,
        dma((2,)),
        dma((n - 1,)),
        dma((n - 1,)),
        dma((n,)),
        dma((n,)),
    ]
    results = pl.pallas_call(
        functools.partial(kernel, n, segs, nb, dim, nhop, cap),
        out_shape=(
            jax.ShapeDtypeStruct(amplitudes.shape, F32),
            jax.ShapeDtypeStruct(amplitudes.shape, F32),
            jax.ShapeDtypeStruct((1, 2), F32),
        ),
        in_specs=[hbm] * 5 + [smem] * 5,
        out_specs=(any_space, any_space, vmem),
        scratch_shapes=scratch,
        compiler_params=pltpu.CompilerParams(
            collective_id=0, has_side_effects=True, vmem_limit_bytes=60 * 1024 * 1024
        ),
    )(
        amplitudes, left_env, right_env, hop_left, hop_right,
        charges.T, dims.T, kept, fetch.transpose(0, 2, 1), slots,
    )
    return pl.pallas_call(
        finish,
        out_shape=[jax.ShapeDtypeStruct(r.shape, r.dtype) for r in results],
        in_specs=[any_space] * 3,
        out_specs=[any_space] * 3,
        scratch_shapes=[dma((3,))],
    )(*results)


def solution(mesh):
    placed = (
        P(("job", "seg"), "blk", None, None),
        P(("job", "seg"), "blk", None, None),
        P(("job", "seg"), "blk", None, None),
        P(("job", "seg"), "blk", None, None, None),
        P(("job", "seg"), "blk", None, None, None),
        P("job", None),
        P(("job", "blk"), None),
        P(("job", "blk")),
        P("job", None, None),
        P(("job", "blk"), None),
    )
    return jax.shard_map(
        functools.partial(on_device, mesh.shape["blk"], mesh.shape["seg"]),
        mesh=mesh,
        in_specs=placed,
        out_specs=(
            P(("job", "seg"), "blk", None, None),
            P(("job", "seg"), "blk", None, None),
            P(("job", "seg"), None),
        ),
        check_vma=False,
    )
```

time: 69 us -> 72.7 us (1.054)
  Pallas kernels: 56.7 us -> 71.9 us
  local copies, waits for them, and re-layouts: 11.2 us -> 0 us
    pallas_call x0 -> x1, Pallas kernels: none -> 17 us  [on_device(): pl.pallas_call(finish, out_shape=[jax.ShapeDtypeStruct(r.shape, r.dtype)...]
    unnamed x20 -> x0, local copies, waits for them, and re-layouts: 11.2 us -> none
    pallas_call x1, Pallas kernels: 56.7 us -> 54.9 us  [on_device(): pl.pallas_call(functools.partial(kernel, n, segs, nb, dim, nhop, cap), ou...]
where the time goes in v2:
time: 72.7 us; the launch traced here: 72.5 us
  Pallas kernels  71.9 us (99%)
    pallas_call x1, Pallas kernels, on_device(): pl.pallas_call(functools.partial(kernel, n, segs, nb, dim, nhop, cap), ou...  54.9 us
    pallas_call x1, Pallas kernels, on_device(): pl.pallas_call(finish, out_shape=[jax.ShapeDtypeStruct(r.shape, r.dtype)...  17 us

profile of v2, /device:TPU:0, one launch (start us, length us, event | category | flops | bytes accessed | tf_op | source)
XLA Modules:
  0.0 72.5 jit_solution(8586968911413312670)
XLA Ops:
  0.6 54.9 %shard_map.121 = (f32[1,4,128,128]{3,2,1,0:T(8,128)}, f32[1,4,128,128]{3,2,1,0:T(8,128)}, f32[1,2]{1,0:T(1,128)}) custom-call(f32[1,4,128,128]{3,2,1,0:T(8,128)} %amp_hbm.1, f32[1,4,128,128]{3,2,1,0:T(8,128)} %left_hbm.1, f32[1,4,128,128]{3,2,1,0:T(8,128)} %right_hbm.1, bf16[1,4,12,128,128]{4,3,2,1,0:T(8,128)(2,1)} %hopl_hbm.1, ...), custom_call_target="tpu_custom_call" | custom-call | tf_op jit(solution)/shard_map/pallas_call | solution.py:460
  55.5 17.0 %shard_map.122 = (f32[1,4,128,128]{3,2,1,0:T(8,128)}, f32[1,4,128,128]{3,2,1,0:T(8,128)}, f32[1,2]{1,0:T(1,128)}) custom-call(f32[1,4,128,128]{3,2,1,0:T(8,128)} %get-tuple-element.6.wave, f32[1,4,128,128]{3,2,1,0:T(8,128)} %get-tuple-element.7.bound, f32[1,2]{1,0:T(1,128)} %get-tuple-element.8.energy), custom_call_target="tpu_custom_call" | custom-call | tf_op jit(solution)/shard_map/pallas_call | solution.py:477

commit v3 on v2

--- a/solution.py
+++ b/solution.py
@@ -56,7 +56,7 @@
     seg_prev = lax.rem(seg + segs - 1, segs)
     peers = [lax.rem(me + d, n) for d in range(1, n)]
     group = [lax.rem(me + d, n) for d in range(n)]
-    order = sorted(range(n - 1), key=lambda i: -min(i + 1, n - 1 - i))
+    order = sorted(range(n - 1), key=lambda i: min(i + 1, n - 1 - i))
     entries = float(n * nb * dim * dim)
 
     loads = [
@@ -392,15 +392,10 @@
     wave_out.wait()
 
 
-def finish(wave, bound, energy, wave_hbm, bound_hbm, energy_hbm, sems):
-    copies = [
-        pltpu.make_async_copy(src, dst, sems.at[i])
-        for i, (src, dst) in enumerate([(wave, wave_hbm), (bound, bound_hbm), (energy, energy_hbm)])
-    ]
-    for copy in copies:
-        copy.start()
-    for copy in copies:
-        copy.wait()
+def finish(wave, bound, energy, wave_out, bound_out, energy_out):
+    wave_out[...] = wave[...]
+    bound_out[...] = bound[...]
+    energy_out[...] = energy[...]
 
 
 def on_device(n, segs, *args):
@@ -477,9 +472,8 @@
     return pl.pallas_call(
         finish,
         out_shape=[jax.ShapeDtypeStruct(r.shape, r.dtype) for r in results],
-        in_specs=[any_space] * 3,
-        out_specs=[any_space] * 3,
-        scratch_shapes=[dma((3,))],
+        in_specs=[vmem] * 3,
+        out_specs=[vmem] * 3,
     )(*results)
 
 

time: 72.7 us -> 55.9 us (0.77)
  Pallas kernels: 71.9 us -> 55.1 us
    pallas_call x1, Pallas kernels: 17 us -> 1.84 us  [on_device(): pl.pallas_call(finish, out_shape=[jax.ShapeDtypeStruct(r.shape, r.dtype)...]
    pallas_call x1, Pallas kernels: 54.9 us -> 53.2 us  [on_device(): pl.pallas_call(functools.partial(kernel, n, segs, nb, dim, nhop, cap), ou...]
where the time goes in v3:
time: 55.9 us; the launch traced here: 55.7 us
  Pallas kernels  55.1 us (99%)
  between operations  0.64 us (1%)
    pallas_call x1, Pallas kernels, on_device(): pl.pallas_call(functools.partial(kernel, n, segs, nb, dim, nhop, cap), ou...  53.2 us
    pallas_call x1, Pallas kernels, on_device(): pl.pallas_call(finish, out_shape=[jax.ShapeDtypeStruct(r.shape, r.dtype)...  1.84 us

profile of v3, /device:TPU:0, one launch (start us, length us, event | category | flops | bytes accessed | tf_op | source)
XLA Modules:
  0.0 55.7 jit_solution(14346258565709992654)
XLA Ops:
  0.6 53.2 %shard_map.121 = (f32[1,4,128,128]{3,2,1,0:T(8,128)}, f32[1,4,128,128]{3,2,1,0:T(8,128)}, f32[1,2]{1,0:T(1,128)}) custom-call(f32[1,4,128,128]{3,2,1,0:T(8,128)} %amp_hbm.1, f32[1,4,128,128]{3,2,1,0:T(8,128)} %left_hbm.1, f32[1,4,128,128]{3,2,1,0:T(8,128)} %right_hbm.1, bf16[1,4,12,128,128]{4,3,2,1,0:T(8,128)(2,1)} %hopl_hbm.1, ...), custom_call_target="tpu_custom_call" | custom-call | tf_op jit(solution)/shard_map/pallas_call | solution.py:455
  53.9 1.8 %shard_map.122 = (f32[1,4,128,128]{3,2,1,0:T(8,128)}, f32[1,4,128,128]{3,2,1,0:T(8,128)}, f32[1,2]{1,0:T(1,128)}) custom-call(f32[1,4,128,128]{3,2,1,0:T(8,128)} %get-tuple-element.6.wave, f32[1,4,128,128]{3,2,1,0:T(8,128)} %get-tuple-element.7.bound, f32[1,2]{1,0:T(1,128)} %get-tuple-element.8.energy), custom_call_target="tpu_custom_call" | custom-call | tf_op jit(solution)/shard_map/pallas_call | solution.py:472
